TPU v7x, 32 devices: a whole 2x2x4 slice. The times are simulated.
32 devices in a mesh: dp: 4 (over y, x), seq: 4 (over z), heads: 2 (over core).
Axes of the slice: x: 2, y: 2, z: 4, core: 2. Of those that a mesh axis runs over, the one named last changes fastest.
Arguments:
- tokens: bfloat16 [4, 4096, 1024], P('dp', ('seq', 'heads')), may hold values from -6 to 6
- cotangent: bfloat16 [4, 4096, 1024], P('dp', ('seq', 'heads')), may hold values from -6 to 6
- qkvu_weight: bfloat16 [1024, 4, 1024], P(None, None, 'heads'), may hold values from -0.1875 to 0.1875
- out_weight: bfloat16 [1024, 1024], P('heads'), may hold values from -0.1875 to 0.1875
- up_weight: bfloat16 [1024, 2816], replicated, may hold values from -0.1875 to 0.1875
- gate_weight: bfloat16 [1024, 2816], replicated, may hold values from -0.1875 to 0.1875
- down_weight: bfloat16 [2816, 1024], replicated, may hold values from -0.109375 to 0.109375
- decay_rate: float32 [8], P('heads'), may hold values from 4.8828126e-05 to 0.02
- item_length: int32 [4], replicated, may hold values from 1024 to 4096, as said below
- item_slot: int32 [4], replicated, may hold values from 0 to 3, each once
Outputs:
- block_output: bfloat16 [4, 4096, 1024], P('dp', ('seq', 'heads'))
- input_grad: float32 [4, 4096, 1024], P('dp', ('seq', 'heads'))
- qkvu_grad: float32 [1024, 4, 1024], P(None, None, 'heads')
- out_grad: float32 [1024, 1024], P('heads')
- up_grad: float32 [1024, 2816], P(None, 'heads')
- gate_grad: float32 [1024, 2816], P(None, 'heads')
- down_grad: float32 [2816, 1024], P('heads')
Inputs may be any that keep to these rules, and one draw needn't show every extreme that they name: `item_length`: an item's valid positions are its first ones; at least one item fills all 4096 positions. `item_slot`: each item stands at exactly one index of dp.
All inputs are finite; a program needn't handle non-finite values.
Results may differ from a plain program's by a relative error of at most 0.012.
Values may be sent and summed in bfloat16 or wider, within the bound.
No kernel may reach another device: no remote copies, remote signals or barrier semaphores. Data moves between devices by JAX's collectives and lax.ppermute only.
A program may use at most 256 MiB of HBM per device.

v0:
```python
import jax
import jax.numpy as jnp
from jax import lax
from jax.sharding import PartitionSpec as P

ATT_BLOCK = 512


epsilon = 1e-06
highest = lax.Precision.HIGHEST


def prefix(value, axis, join, neutral, backward):
    count, mine = (lax.axis_size(axis), lax.axis_index(axis))
    pieces = jax.tree.map(lambda part: lax.all_gather(part, axis), value)
    if backward:
        pieces = jax.tree.map(lambda part: part[::-1], pieces)
        mine = count - 1 - mine
    total = jax.tree.map(
        lambda part, zero: jnp.full_like(part, 0) + jnp.asarray(zero, part.dtype), value, neutral
    )

    def turn(position, total):
        longer = join(total, jax.tree.map(lambda part: part[position], pieces))
        return jax.tree.map(lambda new, old: jnp.where(position < mine, new, old), longer, total)

    return lax.fori_loop(0, count - 1, turn, total)


def simple_norm(value):
    scale = lax.rsqrt(jnp.mean(value * value, axis=-1, keepdims=True) + epsilon)
    return (value * scale, scale)


def norm_back(value, scale, grad):
    return scale * grad - value * (scale * scale * scale) * jnp.mean(
        value * grad, axis=-1, keepdims=True
    )


def swish(value):
    return value * jax.nn.sigmoid(value)


def swish_slope(value):
    sigmoid_part = jax.nn.sigmoid(value)
    return sigmoid_part * (1.0 + value * (1.0 - sigmoid_part))


def rotation(positions, half_dim):
    frequency = 10000.0 ** (-jnp.arange(half_dim, dtype=jnp.float32) / half_dim)
    angles = positions[:, None] * frequency[None, :]
    return (jnp.cos(angles)[:, None, :], jnp.sin(angles)[:, None, :])


def rotate(value, cosine, sine_part, inverse):
    half_dim = value.shape[-1] // 2
    first_half = value[..., :half_dim]
    second_half = value[..., half_dim:]
    if inverse:
        return jnp.concatenate(
            [
                first_half * cosine + second_half * sine_part,
                second_half * cosine - first_half * sine_part,
            ],
            axis=-1,
        )
    return jnp.concatenate(
        [
            first_half * cosine - second_half * sine_part,
            first_half * sine_part + second_half * cosine,
        ],
        axis=-1,
    )


def attention_tables(rates, block):
    offsets = jnp.arange(block, dtype=jnp.float32)
    spread = offsets[:, None] - offsets[None, :]
    decay_matrix = jnp.where(
        spread[None] >= 0.0, jnp.exp(-rates[:, None, None] * jnp.maximum(spread, 0.0)[None]), 0.0
    )
    entering = jnp.exp(-rates[None, :] * (offsets[:, None] + 1.0))
    leaving = jnp.exp(-rates[None, :] * (block - 1.0 - offsets[:, None]))
    carried = jnp.exp(-rates * block)
    return (decay_matrix, entering, leaving, carried)


def combine_states(earlier, later):
    return (earlier[0] * later[0], later[0][:, None, None] * earlier[1] + later[1])


def select_entry(table, index):
    return jnp.sum(jnp.where(jnp.arange(table.shape[0]) == index, table, 0))


def attend_forward(queries, keys, values, rates, block):
    seq_rows, local_heads, head_dim = queries.shape
    blocks = seq_rows // block
    decay_matrix, entering, leaving, carried = attention_tables(rates, block)
    query_blocks = queries.reshape(blocks, block, local_heads, head_dim)
    key_blocks = keys.reshape(blocks, block, local_heads, head_dim)
    value_blocks = values.reshape(blocks, block, local_heads, head_dim)
    scaled_keys = (key_blocks.astype(jnp.float32) * leaving[None, :, :, None]).astype(jnp.bfloat16)
    contrib = jnp.einsum(
        "nshd,nshe->nhde", scaled_keys, value_blocks, preferred_element_type=jnp.float32
    )
    block_index = jnp.arange(blocks, dtype=jnp.float32)
    powers = jnp.exp(-rates[None, :] * block * (blocks - 1.0 - block_index[:, None]))
    local_state = jnp.sum(powers[:, :, None, None] * contrib, axis=0)
    device_decay = jnp.exp(-rates * seq_rows)
    identity = (jnp.ones_like(rates), jnp.zeros_like(local_state))
    decay_in, state_in = prefix((device_decay, local_state), "seq", combine_states, identity, False)

    def step(state, inputs):
        query_part, key_part, value_part, contrib_part = inputs
        scores = jnp.einsum(
            "thd,shd->hts", query_part, key_part, preferred_element_type=jnp.float32
        )
        weights = (scores * decay_matrix).astype(jnp.bfloat16)
        inner = jnp.einsum("hts,shd->thd", weights, value_part, preferred_element_type=jnp.float32)
        outer = entering[:, :, None] * jnp.einsum(
            "thd,hde->the",
            query_part,
            state.astype(jnp.bfloat16),
            preferred_element_type=jnp.float32,
        )
        return (carried[:, None, None] * state + contrib_part, (inner + outer, state))

    final_state, (outputs, states) = lax.scan(
        step, state_in, (query_blocks, key_blocks, value_blocks, contrib)
    )
    return (outputs.reshape(seq_rows, local_heads, head_dim), states, scaled_keys)


def attend_backward(queries, keys, values, rates, block, states, scaled_keys, out_grads):
    seq_rows, local_heads, head_dim = queries.shape
    blocks = seq_rows // block
    decay_matrix, entering, leaving, carried = attention_tables(rates, block)
    query_blocks = queries.reshape(blocks, block, local_heads, head_dim)
    key_blocks = keys.reshape(blocks, block, local_heads, head_dim)
    value_blocks = values.reshape(blocks, block, local_heads, head_dim)
    grad_blocks = out_grads.reshape(blocks, block, local_heads, head_dim)
    scaled_grads = entering[None, :, :, None] * grad_blocks.astype(jnp.float32)
    direct = jnp.einsum(
        "nthd,nthe->nhde", query_blocks.astype(jnp.float32), scaled_grads, precision=highest
    )
    block_index = jnp.arange(blocks, dtype=jnp.float32)
    powers = jnp.exp(-rates[None, :] * block * block_index[:, None])
    total_direct = jnp.sum(powers[:, :, None, None] * direct, axis=0)
    device_decay = jnp.exp(-rates * seq_rows)
    identity = (jnp.ones_like(rates), jnp.zeros_like(total_direct))
    decay_out, grad_out = prefix(
        (device_decay, total_direct), "seq", combine_states, identity, True
    )

    def step(carry, inputs):
        (
            query_part,
            key_part,
            value_part,
            grad_part,
            scaled_part,
            keys_scaled,
            state,
            direct_part,
        ) = inputs
        value_wide = value_part.astype(jnp.float32)
        grad_scaled_keys = jnp.einsum("she,hde->shd", value_wide, carry, precision=highest)
        value_from_state = jnp.einsum(
            "shd,hde->she", keys_scaled.astype(jnp.float32), carry, precision=highest
        )
        scores = jnp.einsum(
            "thd,shd->hts", query_part, key_part, preferred_element_type=jnp.float32
        )
        weights = (scores * decay_matrix).astype(jnp.bfloat16)
        value_grad = (
            jnp.einsum("hts,thd->shd", weights, grad_part, preferred_element_type=jnp.float32)
            + value_from_state
        )
        score_grad = jnp.einsum(
            "thd,shd->hts", grad_part, value_part, preferred_element_type=jnp.float32
        )
        score_grad = (score_grad * decay_matrix).astype(jnp.bfloat16)
        state_low = state.astype(jnp.bfloat16).astype(jnp.float32)
        query_grad = jnp.einsum(
            "hts,shd->thd", score_grad, key_part, preferred_element_type=jnp.float32
        ) + jnp.einsum("the,hde->thd", scaled_part, state_low, precision=highest)
        key_grad = (
            jnp.einsum("hts,thd->shd", score_grad, query_part, preferred_element_type=jnp.float32)
            + grad_scaled_keys * leaving[:, :, None]
        )
        new_carry = carried[:, None, None] * carry + direct_part
        return (new_carry, (query_grad, key_grad, value_grad))

    inputs = (
        query_blocks,
        key_blocks,
        value_blocks,
        grad_blocks,
        scaled_grads,
        scaled_keys,
        states,
        direct,
    )
    first_carry, (query_grads, key_grads, value_grads) = lax.scan(
        step, grad_out, inputs, reverse=True
    )
    shape = (seq_rows, local_heads, head_dim)
    return (query_grads.reshape(shape), key_grads.reshape(shape), value_grads.reshape(shape))


def shards(
    tokens,
    cotangent,
    qkvu_weight,
    out_weight,
    up_weight,
    gate_weight,
    down_weight,
    decay_rate,
    item_length,
    item_slot,
):
    head_count = lax.axis_size("heads")
    inputs = tokens[0].astype(jnp.float32)
    rows, width = inputs.shape
    seq_rows = rows * head_count
    local_heads = decay_rate.shape[0]
    head_dim = qkvu_weight.shape[2] // local_heads
    half_dim = head_dim // 2
    seq_place = lax.axis_index("seq")
    head_place = lax.axis_index("heads")
    data_place = lax.axis_index("dp")
    slot_here = select_entry(item_slot, data_place)
    length_here = select_entry(item_length, slot_here)
    token_index = seq_place * seq_rows + head_place * rows + jnp.arange(rows, dtype=jnp.int32)
    valid = (token_index < length_here).astype(jnp.float32)[:, None]
    normed, scale_one = simple_norm(inputs)
    normed_low = normed.astype(jnp.bfloat16)
    gathered, full_out = (
        lax.all_gather(normed_low, "heads", axis=0, tiled=True),
        lax.all_gather(out_weight, "heads", axis=0, tiled=True),
    )
    flat_qkvu = qkvu_weight.reshape(width, 4 * local_heads * head_dim)
    projected = jnp.dot(gathered, flat_qkvu, preferred_element_type=jnp.float32).reshape(
        seq_rows, 4, local_heads, head_dim
    )
    head_positions = (seq_place * seq_rows + jnp.arange(seq_rows, dtype=jnp.int32)).astype(
        jnp.float32
    )
    cosine, sine_part = rotation(head_positions, half_dim)
    queries = rotate(swish(projected[:, 0]), cosine, sine_part, False).astype(jnp.bfloat16)
    keys = rotate(swish(projected[:, 1]), cosine, sine_part, False).astype(jnp.bfloat16)
    values = swish(projected[:, 2]).astype(jnp.bfloat16)
    gate_low = projected[:, 3].reshape(seq_rows, local_heads * head_dim).astype(jnp.bfloat16)
    attended, states, scaled_keys = attend_forward(queries, keys, values, decay_rate, ATT_BLOCK)
    attended_low = attended.reshape(seq_rows, local_heads * head_dim).astype(jnp.bfloat16)
    arrived, gate_here = (
        lax.all_to_all(attended_low, "heads", split_axis=0, concat_axis=1, tiled=True),
        lax.all_to_all(gate_low, "heads", split_axis=0, concat_axis=1, tiled=True),
    )
    arrived_wide = arrived.astype(jnp.float32)
    gate_wide = gate_here.astype(jnp.float32)
    attn_norm, scale_two = simple_norm(arrived_wide)
    mixed = (attn_norm * gate_wide).astype(jnp.bfloat16)
    hidden = inputs + jnp.dot(mixed, full_out, preferred_element_type=jnp.float32)
    normed_two, scale_three = simple_norm(hidden)
    normed_two_low = normed_two.astype(jnp.bfloat16)
    left = jnp.dot(normed_two_low, up_weight, preferred_element_type=jnp.float32)
    right = jnp.dot(normed_two_low, gate_weight, preferred_element_type=jnp.float32)
    inner_low = (left * right).astype(jnp.bfloat16)
    result = (hidden + jnp.dot(inner_low, down_weight, preferred_element_type=jnp.float32)) * valid
    grad_result = cotangent[0].astype(jnp.float32) * valid
    grad_low = grad_result.astype(jnp.bfloat16)
    grad_down = jnp.dot(inner_low.T, grad_low, preferred_element_type=jnp.float32)
    grad_inner = jnp.dot(grad_low, down_weight.T, preferred_element_type=jnp.float32)
    grad_left = (grad_inner * right).astype(jnp.bfloat16)
    grad_right = (grad_inner * left).astype(jnp.bfloat16)
    grad_up = jnp.dot(normed_two_low.T, grad_left, preferred_element_type=jnp.float32)
    grad_gate = jnp.dot(normed_two_low.T, grad_right, preferred_element_type=jnp.float32)
    grad_normed_two = jnp.dot(grad_left, up_weight.T, preferred_element_type=jnp.float32) + jnp.dot(
        grad_right, gate_weight.T, preferred_element_type=jnp.float32
    )
    grad_hidden = grad_result + norm_back(hidden, scale_three, grad_normed_two)
    grad_branch = grad_hidden.astype(jnp.bfloat16)
    grad_out = jnp.dot(mixed.T, grad_branch, preferred_element_type=jnp.float32)
    grad_mixed = jnp.dot(grad_branch, full_out.T, preferred_element_type=jnp.float32)
    grad_gate_u = (grad_mixed * attn_norm).astype(jnp.bfloat16)
    grad_arrived = norm_back(arrived_wide, scale_two, grad_mixed * gate_wide).astype(jnp.bfloat16)
    grad_attended, grad_gate_heads = (
        lax.all_to_all(grad_arrived, "heads", split_axis=1, concat_axis=0, tiled=True),
        lax.all_to_all(grad_gate_u, "heads", split_axis=1, concat_axis=0, tiled=True),
    )
    query_grad, key_grad, value_grad = attend_backward(
        queries,
        keys,
        values,
        decay_rate,
        ATT_BLOCK,
        states,
        scaled_keys,
        grad_attended.reshape(seq_rows, local_heads, head_dim),
    )
    query_grad_low = query_grad.astype(jnp.bfloat16)
    key_grad_low = key_grad.astype(jnp.bfloat16)
    value_grad_low = value_grad.astype(jnp.bfloat16)
    grad_pre_q = (
        swish_slope(projected[:, 0])
        * rotate(query_grad_low.astype(jnp.float32), cosine, sine_part, True)
    ).astype(jnp.bfloat16)
    grad_pre_k = (
        swish_slope(projected[:, 1])
        * rotate(key_grad_low.astype(jnp.float32), cosine, sine_part, True)
    ).astype(jnp.bfloat16)
    grad_pre_v = (swish_slope(projected[:, 2]) * value_grad_low.astype(jnp.float32)).astype(
        jnp.bfloat16
    )
    grad_pre_u = grad_gate_heads.reshape(seq_rows, local_heads, head_dim)
    grad_proj = jnp.stack([grad_pre_q, grad_pre_k, grad_pre_v, grad_pre_u], axis=1).reshape(
        seq_rows, 4 * local_heads * head_dim
    )
    grad_normed = lax.psum_scatter(
        jnp.dot(grad_proj, flat_qkvu.T, preferred_element_type=jnp.float32),
        "heads",
        scatter_dimension=0,
        tiled=True,
    )
    qkvu_share = jnp.dot(gathered.T, grad_proj, preferred_element_type=jnp.float32).reshape(
        width, 4, local_heads * head_dim
    )
    up_share, gate_share, down_share, out_share = (
        lax.psum_scatter(grad_up, "heads", scatter_dimension=1, tiled=True),
        lax.psum_scatter(grad_gate, "heads", scatter_dimension=1, tiled=True),
        lax.psum_scatter(grad_down, "heads", scatter_dimension=0, tiled=True),
        lax.psum_scatter(grad_out, "heads", scatter_dimension=0, tiled=True),
    )
    grad_inputs = grad_hidden + norm_back(inputs, scale_one, grad_normed)
    totals = lax.psum((up_share, gate_share, down_share, out_share, qkvu_share), ("dp", "seq"))
    output = result.astype(jnp.bfloat16)[None]
    return (output, grad_inputs[None], totals[4], totals[3], totals[0], totals[1], totals[2])


def solution(mesh):
    placed = (
        P("dp", ("seq", "heads"), None),
        P("dp", ("seq", "heads"), None),
        P(None, None, "heads"),
        P("heads", None),
        P(),
        P(),
        P(),
        P("heads"),
        P(),
        P(),
    )
    return jax.shard_map(
        shards,
        mesh=mesh,
        in_specs=placed,
        out_specs=(
            P("dp", ("seq", "heads"), None),
            P("dp", ("seq", "heads"), None),
            P(None, None, "heads"),
            P("heads", None),
            P(None, "heads"),
            P(None, "heads"),
            P("heads", None),
        ),
        check_vma=False,
    )
```

profile of v0, /device:TPU:0, one launch (start us, length us, event | category | flops | bytes accessed | tf_op | source)
XLA Modules:
  0.0 1086.8 jit_solution(1072247755166594141)
XLA Ops:
  11.8 5.6 copy.128
  17.4 6.5 copy.75
  26.6 7.2 fusion.97
  60.2 13.7 %all-reduce = f32[16]{0:T(128)S(1)} all-reduce(f32[16]{0:T(128)S(1)} %get-tuple-element.982), channel_id=2, replica_groups=mesh['dp'=4,'seq'=4,'heads'=2] {'seq'}, use_global_device_ids=true, to_apply=%add | all-reduce | flops 16 | bytes 128
  92.5 15.5 %while.68 = (s32[]{:T(128)}, f32[4,128,128]{2,1,0:T(8,128)S(1)}, bf16[2,512,4,128]{1,3,2,0:T(8,128)(2,1)}, bf16[2,4,128,128]{3,2,1,0:T(8,128)(2,1)}, f32[4]{0:T(...) while((s32[]{:T(128)}, f32[4,128,128]{2,1,0:T(8,128)S(1)}, ...), condition=%wide.region_5.6_spmd.clone.clone, body=%wide.region_4.5_spmd.clone.clone.sunk | while | flops 608897024 | bytes 10245329 | solution.py:130
  110.3 5.7 all_to_all.53
  122.8 8.9 fusion.124
  131.7 4.9 fusion.123
  136.6 9.0 multiply_convert_fusion
  145.6 6.2 fusion.125
  151.9 5.5 multiply_reduce_fusion.1
  164.7 13.0 %all_to_all.54 = bf16[512,2,512]{0,2,1:T(8,128)(2,1)S(1)} all-to-all(bf16[512,2,512]{0,2,1:T(8,128)(2,1)S(1)} %bitcast.357), channel_id=1, replica_groups=mesh['dp'=4,'seq'=4,'heads'=2] {'heads'}, dimensions={1} | all-to-all | bytes 2097152 | tf_op jit(solution)/shard_map/all_to_all | solution.py:292
  186.2 9.7 fusion.114
  195.9 9.6 fusion.128
  205.6 9.5 fusion.127
  217.5 6.2 all_to_all.55
  239.9 34.4 %while.69 = (s32[]{:T(128)}, f32[4,128,128]{2,1,0:T(8,128)S(1)}, bf16[2,512,4,128]{1,3,2,0:T(8,128)(2,1)}, bf16[2,512,4,128]{1,3,2,0:T(8,128)(2,1)}, bf16[2,512,...) while((s32[]{:T(128)}, f32[4,128,128]{2,1,0:T(8,128)S(1)}, ...), condition=%wide.region_16.17_spmd.clone.clone, body=%wide.region_15.16_spmd.clone.clone.sunk | while | flops 2559707136 | bytes 67528216 | solution.py:206
  288.9 5.1 fusion.93
  297.8 6.1 fusion.126
  304.1 11.4 %fusion.99 = f32[1024,4,512]{2,0,1:T(8,128)} fusion(bf16[4,512,1024]{2,1,0:T(8,128)(2,1)} %bitcast.355, bf16[1024,1024]{1,0:T(8,128)(2,1)} %all-gather.8.cloned.1.call-done), kind=kOutput, calls=%fused_computation.116 | convolution fusion | flops 4294967296 | bytes 14680064 | tf_op jit(solution)/shard_map/dot_general | solution.py:329
  315.6 8.5 fusion.107
  328.1 725.2 %all-reduce.4.cloned.1.call-done = (f32[1024,4,512]{2,0,1:T(8,128)}, f32[512,1024]{1,0:T(8,128)}, f32[1024,1408]{1,0:T(8,128)}, f32[1024,1408]{1,0:T(8,128)}, f32[1408,1024]{1,0:T(8,128)}) async-done(((f32[1024,4,512]{2,0,1:T(8,128)}, f32[512,1024]{1,0:T(8,128)}, f32[1024,1408]{1,0:T(8,128)}, f32[1024,1408]{1,0:T(8,128)}, f32[1408,1024]{1,0:T(8,128)}), (f32[1024,4,512]{2,0,1:T(8,128)}, ...) | async-done | bytes 27787280 | tf_op jit(solution)/shard_map/psum | solution.py:339
  1053.3 12.3 %copy.101 = f32[1024,4,512]{2,1,0:T(4,128)} copy(f32[1024,4,512]{2,0,1:T(8,128)} %get-tuple-element.942) | data formatting | bytes 16777216
  1067.0 6.1 copy.188
  (289 shorter events, 181.6 us)
Async XLA Ops:
  7.2 19.4 %all-gather.8.cloned.1.call-start = ((), (), s32[]{:S(2)}) async-start(), calls=%async_computation.9 | async-start | bytes 3145728 | tf_op jit(solution)/shard_map/all_gather | solution.py:242
  9.3 8.1 copy-start.42
  11.8 76.4 %all-gather.12.cloned.1.call-start = ((), (), s32[]{:S(2)}) async-start(), calls=%async_computation.16 | async-start | bytes 1310720 | tf_op jit(solution)/shard_map/all_gather | solution.py:15
  17.4 7.8 copy-start.45
  26.5 22.9 %copy-start.33 = (f32[1024,64]{0,1:T(8,128)}, f32[1024,64]{0,1:T(8,128)S(1)}, u32[]{:S(2)}) copy-start(f32[1024,64]{0,1:T(8,128)S(1)} %get-tuple-element.969) | copy-start | bytes 786436
  26.5 22.9 %copy-start.35 = (f32[1024,64]{0,1:T(8,128)}, f32[1024,64]{0,1:T(8,128)S(1)}, u32[]{:S(2)}) copy-start(f32[1024,64]{0,1:T(8,128)S(1)} %get-tuple-element.970) | copy-start | bytes 786436
  55.2 18.8 %copy-start.46 = (s32[4]{0:T(128)S(1)}, s32[4]{0:T(128)}, u32[]{:S(2)}) copy-start(s32[4]{0:T(128)} %param.27) | copy-start | bytes 52
  55.2 19.4 %copy-start.47 = (s32[4]{0:T(128)S(1)}, s32[4]{0:T(128)}, u32[]{:S(2)}) copy-start(s32[4]{0:T(128)} %param.26) | copy-start | bytes 52
  57.2 61.7 %all-gather.10.cloned.1.call-start = ((), (), s32[]{:S(2)}) async-start(), calls=%async_computation.10 | async-start | bytes 3145728 | tf_op jit(solution)/shard_map/all_gather | solution.py:243
  58.0 173.1 %all-gather.14.cloned.1.call-start = ((), (), s32[]{:S(2)}) async-start(), calls=%async_computation.17 | async-start | bytes 1310720 | tf_op jit(solution)/shard_map/all_gather | solution.py:15
  122.5 34.9 %copy-start.17 = (f32[512,1024]{1,0:T(8,128)}, f32[512,1024]{1,0:T(8,128)S(1)}, u32[]{:S(2)}) copy-start(f32[512,1024]{1,0:T(8,128)S(1)} %get-tuple-element.988) | copy-start | bytes 6291460
  122.5 9.1 slice-start.4
  122.7 8.9 copy-start.40
  122.7 8.9 slice-start.5
  122.7 13.9 %slice-start.2 = ((s8[5767168]{0:T(1024)(128)(4,1)}), s8[4194304]{0:T(1024)(128)(4,1)S(1)}, s32[]{:S(2)}) async-start(s8[5767168]{0:T(1024)(128)(4,1)} %bitcast.350), calls=%async_computation.21 | async-start | bytes 8388608
  181.6 134.0 %reduce-scatter.8.cloned.1.call-start = ((), (), s32[]{:S(2)}) async-start(), calls=%async_computation.12 | async-start | bytes 6291456 | tf_op jit(solution)/shard_map/reduce_scatter | solution.py:336
  186.1 129.4 %reduce-scatter.14.cloned.1.call-start = ((), (), s32[]{:S(2)}) async-start(), calls=%async_computation.15 | async-start | bytes 17301504 | tf_op jit(solution)/shard_map/reduce_scatter | solution.py:335
  195.9 119.6 %reduce-scatter.12.cloned.1.call-start = ((), (), s32[]{:S(2)}) async-start(), calls=%async_computation.14 | async-start | bytes 17301504 | tf_op jit(solution)/shard_map/reduce_scatter | solution.py:334
  205.5 110.0 %reduce-scatter.10.cloned.1.call-start = ((), (), s32[]{:S(2)}) async-start(), calls=%async_computation.13 | async-start | bytes 17301504 | tf_op jit(solution)/shard_map/reduce_scatter | solution.py:333
  215.1 109.0 %reduce-scatter.6.cloned.1.call-start = ((), (), s32[]{:S(2)}) async-start(), calls=%async_computation.11 | async-start | bytes 6291456 | tf_op jit(solution)/shard_map/reduce_scatter | solution.py:323
  303.9 749.4 %all-reduce.4.cloned.1.call-start = ((), (), s32[]{:S(2)}) async-start(), calls=%async_computation.18 | async-start | bytes 55574528 | tf_op jit(solution)/shard_map/psum | solution.py:339
  315.6 8.5 copy-start.12
  1053.3 12.3 %copy-start.37 = (f32[512,1024]{1,0:T(8,128)S(1)}, f32[512,1024]{1,0:T(8,128)}, u32[]{:S(2)}) copy-start(f32[512,1024]{1,0:T(8,128)} %get-tuple-element.1393) | copy-start | bytes 6291460
  1067.0 9.0 slice-start
  (53 other events, 141.2 us)
Sparse Core Ops, SparseCore 0:
  11.9 13.2 all-gather.7
  57.4 30.7 all-gather.11
  89.8 9.9 all-gather.9
  181.7 27.4 all-gather.13
  211.3 11.5 reduce-scatter.7
  225.1 21.6 reduce-scatter.13
  249.2 21.4 reduce-scatter.11
  273.1 21.4 reduce-scatter.9
  304.0 13.0 reduce-scatter.5
  324.0 729.2 all-reduce.3
where the time goes:
time: 1100 us; the launch traced here: 1090 us
  waiting for transfers between devices  727 us (66%)
  matrix products  151 us (14%)
  local copies, waits for them, and re-layouts  101 us (9%)
  other arithmetic  48.5 us (4%)
  blocking collectives  43.1 us (4%)
  between operations  15.7 us (1%)
    psum x1, waiting for transfers between devices, shards(): lax.psum((up_share, gate_share, down_share, out_share, qkvu_share), ('dp'...  725 us
    unnamed x96, local copies, waits for them, and re-layouts  46.1 us
  transfers between devices with their start and end apart: 10, of which 2 were waited for; matrix products, arithmetic and copies ran while one was open for 16% of the time, Pallas kernels for 0%

commit v1 on v0

v1 whole, which is shorter than its diff:
```python
import functools

import jax
import jax.numpy as jnp
from jax import lax
from jax.experimental import pallas as pl
from jax.experimental.pallas import tpu as pltpu
from jax.sharding import PartitionSpec as P

epsilon = 1e-06
f32 = jnp.float32
bf16 = jnp.bfloat16
CHUNK = 128


def dot(a, b):
    return jnp.dot(a, b, preferred_element_type=f32)


def dot_t(a, b):
    return lax.dot_general(a, b, (((1,), (1,)), ((), ())), preferred_element_type=f32)


def t_dot(a, b):
    return lax.dot_general(a, b, (((0,), (0,)), ((), ())), preferred_element_type=f32)


def whole(value):
    rank = value.ndim
    return pl.BlockSpec(value.shape, lambda i, s: (0,) * rank)


def tiles(value, rows):
    return pl.BlockSpec((rows, value.shape[1]), lambda i, s: (i, 0))


SMEM = pl.BlockSpec(memory_space=pltpu.SMEM)


def call(body, steps, info, ins, outs, scratch=(), after=(), name=None):
    used = len(ins)

    def kernel(info_ref, *refs):
        body(info_ref, *refs[:used], *refs[used + len(after) :])

    return pl.pallas_call(
        kernel,
        grid_spec=pltpu.PrefetchScalarGridSpec(
            num_scalar_prefetch=1,
            grid=(steps,),
            in_specs=[spec for _, spec in ins] + [pl.BlockSpec(memory_space=pl.ANY)] * len(after),
            out_specs=[spec for _, _, spec in outs],
            scratch_shapes=list(scratch),
        ),
        out_shape=[jax.ShapeDtypeStruct(shape, kind) for shape, kind, _ in outs],
        compiler_params=pltpu.CompilerParams(vmem_limit_bytes=52 * 2**20),
        cost_estimate=pl.CostEstimate(flops=0, bytes_accessed=0, transcendentals=0),
        name=name,
    )(info, *[value for value, _ in ins], *after)


def loop(count, step, body):
    def turn(i, _):
        body(pl.ds(pl.multiple_of(i * step, step), step), i * step)
        return 0

    lax.fori_loop(0, count // step, turn, 0)


def head(h, dim):
    return pl.ds(h * dim, dim)


def rotate(value, cosine, sine):
    return value * cosine + pltpu.roll(value, value.shape[1] // 2, 1) * sine


def swish_and_slope(value):
    s = jax.nn.sigmoid(value)
    return value * s, s * (1.0 + value * (1.0 - s))


def row_numbers(start, rows, columns):
    return (lax.broadcasted_iota(jnp.int32, (rows, columns), 0) + start).astype(f32)


def decay_of(rate, start, rows, columns):
    gap = row_numbers(start, rows, columns) - lax.broadcasted_iota(
        jnp.int32, (rows, columns), 1
    ).astype(f32)
    return jnp.where(gap >= 0.0, jnp.exp(-rate * jnp.maximum(gap, 0.0)), 0.0)


def scale_of(total, width):
    return lax.rsqrt(total / width + epsilon)


def row_sum(value):
    return jnp.sum(value, axis=-1, keepdims=True)


def wide(scalar, dim):
    return jnp.full((1, dim), scalar, f32)


def project_kv(block, heads, dim, info, own, other, wk, wv, cs, sn, rate, normed, k, v, sk, sv, contrib, local, pk, pv, kd):
    b = pl.program_id(0)
    mine = b == info[0]
    width = own.shape[1]

    def norm(r, _):
        x = jnp.where(mine, own[r, :].astype(f32), other[r, :].astype(f32))
        normed[r, :] = (x * scale_of(row_sum(x * x), width)).astype(bf16)

    loop(block, 32, norm)
    pk[...] = dot(normed[...], wk[0])
    pv[...] = dot(normed[...], wv[0])

    def act(r, start):
        cosine, sine = cs[r, :], sn[r, :]
        steps = block - 1.0 - row_numbers(start, 64, dim)
        for h in range(heads):
            c = head(h, dim)
            y, slope = swish_and_slope(pk[r, c])
            key = rotate(y, cosine, sine).astype(bf16)
            k[r, c] = key
            sk[r, c] = slope.astype(bf16)
            kd[r, c] = (key.astype(f32) * jnp.exp(-rate[h] * steps)).astype(bf16)
            y, slope = swish_and_slope(pv[r, c])
            v[r, c] = y.astype(bf16)
            sv[r, c] = slope.astype(bf16)

    loop(block, 64, act)
    for h in range(heads):
        c = head(h, dim)
        contrib[b, h] = t_dot(kd[:, c], v[:, c])

    @pl.when(b == 1)
    def _():
        for h in range(heads):
            carried = jnp.exp(wide(-rate[h] * block, dim))
            local[h] = (carried * contrib[0, h] + contrib[1, h]).astype(bf16)


def project_qu(block, heads, dim, info, normed, wq, wu, cs, sn, rate, k, v, q, sq, u, intra, pq):
    pq[...] = dot(normed[...], wq[0])
    u[...] = dot(normed[...], wu[0]).astype(bf16)

    def act(r, start):
        cosine, sine = cs[r, :], sn[r, :]
        for h in range(heads):
            c = head(h, dim)
            y, slope = swish_and_slope(pq[r, c])
            q[r, c] = rotate(y, cosine, sine).astype(bf16)
            sq[r, c] = slope.astype(bf16)

    loop(block, 64, act)
    for h in range(heads):
        c = head(h, dim)
        for start in range(0, block, CHUNK):
            r, upto = pl.ds(start, CHUNK), start + CHUNK
            scores = dot_t(q[r, c], k[:upto, c]) * decay_of(rate[h], start, CHUNK, upto)
            intra[r, c] = dot(scores.astype(bf16), v[:upto, c])


def state_sum(arrived, powers, h, rate, rows, dim):
    total = None
    for part_, power in zip(arrived, powers):
        term = part_[h].astype(f32)
        if power:
            term = term * jnp.exp(wide(-rate[h] * (rows * power), dim))
        total = term if total is None else total + term
    return total


def attend(block, heads, dim, powers, info, q, intra, contrib, rate, *refs):
    arrived, (att, states) = refs[: len(powers)], refs[len(powers) :]
    for h in range(heads):
        c = head(h, dim)
        first = state_sum(arrived, powers, h, rate, 2 * block, dim)
        second = jnp.exp(wide(-rate[h] * block, dim)) * first + contrib[0, h]
        for b, state in enumerate((first, second)):
            states[b, h] = state.astype(bf16)
        for b in range(2):
            state = states[b, h]
            for start in range(0, block, CHUNK):
                r = pl.ds(b * block + start, CHUNK)
                entering = jnp.exp(-rate[h] * (row_numbers(start, CHUNK, dim) + 1.0))
                att[r, c] = (intra[r, c] + entering * dot(q[r, c], state)).astype(bf16)


def begin_back(rows, info, own, other, down, g, grad_inner):
    i = pl.program_id(0)
    mine = (i // 2) == info[0]

    def read(r, start):
        value = jnp.where(mine, own[r, :].astype(f32), other[r, :].astype(f32))
        place = lax.broadcasted_iota(jnp.int32, value.shape, 0) + (start + i * rows)
        g[r, :] = jnp.where(place < info[3], value, 0.0).astype(bf16)

    loop(rows, 32, read)
    grad_inner[...] = dot_t(g[...], down[...]).astype(bf16)


def mix_out(rows, info, att_own, att_other, u_own, u_other, wo_own, wo_other, own, other, hidden, n2, mixed, both):
    mine = (pl.program_id(0) // 2) == info[0]
    half = att_own.shape[1]
    width = 2 * half

    def mix(r, _):
        a, b = att_own[r, :].astype(f32), att_other[r, :].astype(f32)
        scale = scale_of(row_sum(a * a) + row_sum(b * b), width)
        m = (a * scale * u_own[r, :].astype(f32)).astype(bf16)
        mixed[r, :] = m
        both[r, :half] = m
        both[r, half:] = (b * scale * u_other[r, :].astype(f32)).astype(bf16)

    loop(rows, 32, mix)
    hidden[...] = dot(both[:, :half], wo_own[...]) + dot(both[:, half:], wo_other[...])

    def norm(r, _):
        x = jnp.where(mine, own[r, :].astype(f32), other[r, :].astype(f32))
        x = hidden[r, :] + x
        hidden[r, :] = x
        n2[r, :] = (x * scale_of(row_sum(x * x), width)).astype(bf16)

    loop(rows, 32, norm)


def feed(rows, info, n2, up, gate, grad_inner, inner, grad_left, grad_right, left, right):
    left[...] = dot(n2[...], up[...])
    right[...] = dot(n2[...], gate[...])

    def join(r, _):
        a, b, g = left[r, :], right[r, :], grad_inner[r, :].astype(f32)
        inner[r, :] = (a * b).astype(bf16)
        grad_left[r, :] = (g * b).astype(bf16)
        grad_right[r, :] = (g * a).astype(bf16)

    loop(rows, 16, join)


def weight_grad(info, lhs_a, rhs_a, lhs_b, rhs_b, send_a, keep_a, send_b, keep_b):
    step = pl.program_id(0)

    @pl.when(step == 0)
    def _():
        send_a[...] = t_dot(lhs_a[...], rhs_a[...]).astype(bf16)
        send_b[...] = t_dot(lhs_b[...], rhs_b[...]).astype(bf16)

    @pl.when(step == 1)
    def _():
        keep_a[...] = t_dot(lhs_a[...], rhs_a[...]).astype(bf16)
        keep_b[...] = t_dot(lhs_b[...], rhs_b[...]).astype(bf16)


def back_two(info, grad_left, grad_right, up, gate, out):
    out[...] = (dot_t(grad_left[...], up[...]) + dot_t(grad_right[...], gate[...])).astype(bf16)


def split_product(info, inner, down, send, keep):
    result = dot(inner[...], down[...])
    i = pl.program_id(0)

    @pl.when(i < 2)
    def _():
        send[...] = result.astype(bf16)

    @pl.when(i >= 2)
    def _():
        keep[...] = result.astype(bf16)


def back_in(info, du, ga, gb, w, send, keep):
    half = du.shape[1]
    i = pl.program_id(0)
    cut = ga.shape[1] - half
    result = dot_t(ga[:, :half], w[0]) + dot_t(ga[:, half:], w[1, :, :cut])
    result = result + dot_t(gb[:, : half - cut], w[1, :, cut:]) + dot_t(gb[:, half - cut :], w[2])
    result = result + dot_t(du[...], w[3])

    @pl.when(i < 2)
    def _():
        send[...] = result.astype(bf16)

    @pl.when(i >= 2)
    def _():
        keep[...] = result.astype(bf16)


def back_mix(rows, block, heads, dim, info, part_own, part_other, hidden, g, att_own, att_other, u_own, u_other, wo_own, wo_other, q, rate, dh, branch, dgates, datt, direct, local, dm_own, dm_other, es):
    i = pl.program_id(0)
    half = att_own.shape[1]
    width = 2 * half

    def hid(r, _):
        x = hidden[r, :]
        scale = scale_of(row_sum(x * x), width)
        dn = part_own[r, :].astype(f32) + part_other[r, :].astype(f32)
        mean = row_sum(x * dn) / width
        d = g[r, :].astype(f32) + scale * dn - x * (scale * scale * scale * mean)
        dh[r, :] = d
        branch[r, :] = d.astype(bf16)

    loop(rows, 16, hid)
    dm_own[...] = dot_t(branch[...], wo_own[...])
    dm_other[...] = dot_t(branch[...], wo_other[...])

    def att(r, start):
        a, b = att_own[r, :].astype(f32), att_other[r, :].astype(f32)
        scale = scale_of(row_sum(a * a) + row_sum(b * b), width)
        m = dm_own[r, :]
        dgates[r, :] = (m * (a * scale)).astype(bf16)
        da = m * u_own[r, :].astype(f32)
        db = dm_other[r, :] * u_other[r, :].astype(f32)
        mean = (row_sum(a * da) + row_sum(b * db)) / width
        d = (scale * da - a * (scale * scale * scale * mean)).astype(bf16)
        datt[r, :] = d
        place = row_numbers(start + 1, 16, dim) + (lax.rem(i, 2) * rows).astype(f32)
        for h in range(heads):
            c = head(h, dim)
            es[r, c] = (d[:, h * dim : (h + 1) * dim].astype(f32) * jnp.exp(-rate[h] * place)).astype(
                bf16
            )

    loop(rows, 16, att)
    for h in range(heads):
        c = head(h, dim)
        term = t_dot(q[:, c], es[:, c])
        b = i // 2

        @pl.when(lax.rem(i, 2) == 0)
        def _():
            direct[b, h] = term

        @pl.when(lax.rem(i, 2) == 1)
        def _():
            direct[b, h] = direct[b, h] + term

    @pl.when(i == 3)
    def _():
        for h in range(heads):
            carried = jnp.exp(wide(-rate[h] * block, dim))
            local[h] = (direct[0, h] + carried * direct[1, h]).astype(bf16)


def attend_back(block, heads, dim, info, q, k, v, datt, states, sq, cs, sn, rate, gq, dk, dv):
    for h in range(heads):
        c = head(h, dim)
        state = states[0, h]
        for start in reversed(range(0, block, CHUNK)):
            r, upto = pl.ds(start, CHUNK), start + CHUNK
            decay = decay_of(rate[h], start, CHUNK, upto)
            qc, da = q[r, c], datt[r, c]
            weights = (dot_t(qc, k[:upto, c]) * decay).astype(bf16)
            dscore = (dot_t(da, v[:upto, c]) * decay).astype(bf16)
            place = row_numbers(start + 1, CHUNK, dim)
            e = (da.astype(f32) * jnp.exp(-rate[h] * place)).astype(bf16)
            dq = dot(dscore, k[:upto, c]) + dot_t(e, state)
            gq[r, c] = (sq[r, c].astype(f32) * rotate(dq, cs[r, :], -sn[r, :])).astype(bf16)
            dk_term, dv_term = t_dot(dscore, qc), t_dot(weights, da)
            if upto == block:
                dk[:, c] = dk_term
                dv[:, c] = dv_term
            else:
                dk[:upto, c] = dk[:upto, c] + dk_term
                dv[:upto, c] = dv[:upto, c] + dv_term


def finish_back(block, heads, dim, powers, info, k, v, dk, dv, direct, sk, sv, cs, sn, rate, gq, *refs):
    arrived, (out_a, out_b, after) = refs[: len(powers)], refs[len(powers) :]
    b = pl.program_id(0)
    half = heads * dim
    cut = out_a.shape[1] - half

    def put(column, r, value):
        if column < out_a.shape[1]:
            out_a[r, pl.ds(column, dim)] = value
        else:
            out_b[r, pl.ds(column - out_a.shape[1], dim)] = value

    out_a[:, :half] = gq[...]
    for h in range(heads):
        c = head(h, dim)
        last = state_sum(arrived, powers, h, rate, 2 * block, dim)
        before = jnp.exp(wide(-rate[h] * block, dim)) * last + direct[1, h]
        after[...] = jnp.where(b == 1, last, before).astype(bf16)
        for start in range(0, block, CHUNK):
            r = pl.ds(start, CHUNK)
            leaving = jnp.exp(-rate[h] * (block - 1.0 - row_numbers(start, CHUNK, dim)))
            kd = (k[r, c].astype(f32) * leaving).astype(bf16)
            key_grad = dk[r, c] + leaving * dot_t(v[r, c], after[...])
            value_grad = dv[r, c] + dot(kd, after[...])
            gk = sk[r, c].astype(f32) * rotate(key_grad, cs[r, :], -sn[r, :])
            put(half + h * dim, r, gk.astype(bf16))
            put(2 * half + h * dim, r, (sv[r, c].astype(f32) * value_grad).astype(bf16))


def add_quarters(info, keep_a, first_a, second_a, keep_b, first_b, second_b, out):
    cut = keep_a.shape[1]

    def three(x, y, z):
        return (x[...].astype(f32) + y[...].astype(f32) + z[...].astype(f32)).astype(bf16)

    out[:, :cut] = three(keep_a, first_a, second_a)
    out[:, cut:] = three(keep_b, first_b, second_b)


def choose(info, step, pieces, bit_first, bit_second, use):
    first = (step // 2) != bit_first
    second = lax.rem(step, 2) != bit_second
    for index, piece in enumerate(pieces):
        at_first, at_second = index >= 2, index % 2 == 1

        @pl.when((first == at_first) & (second == at_second))
        def _(piece=piece):
            use(piece)


def place_columns(info, *refs):
    out = refs[8]
    step = pl.program_id(0)
    cut = refs[0].shape[1]

    def put_a(piece):
        out[:, :cut] = piece[...].astype(f32)

    def put_b(piece):
        out[:, cut:] = piece[...].astype(f32)

    choose(info, step, refs[:4], info[1], info[2], put_a)
    choose(info, step, refs[4:8], info[2], info[1], put_b)


def place_turned(info, *refs):
    out = refs[8]
    step = pl.program_id(0)
    cut = refs[0].shape[1]

    def put_a(piece):
        out[:cut, :] = piece[...].astype(f32).T

    def put_b(piece):
        out[cut:, :] = piece[...].astype(f32).T

    choose(info, step, refs[:4], info[1], info[2], put_a)
    choose(info, step, refs[4:8], info[2], info[1], put_b)


def place_heads(info, *refs):
    out = refs[12]
    step = pl.program_id(0)
    half = out.shape[2]
    cut = refs[0].shape[1] - half

    def put_a(piece):
        out[:, 0, :] = piece[:, :half].astype(f32)
        out[:, 1, :cut] = piece[:, half:].astype(f32)

    def put_b(piece):
        out[:, 1, cut:] = piece[:, : half - cut].astype(f32)
        out[:, 2, :] = piece[:, half - cut :].astype(f32)

    def put_u(piece):
        out[:, 3, :] = piece[...].astype(f32)

    choose(info, step, refs[:4], info[1], info[2], put_a)
    choose(info, step, refs[4:8], info[2], info[1], put_b)
    choose(info, step, refs[8:12], info[2], info[1], put_u)


def place_rows(info, *refs):
    out = refs[4]

    def put(piece):
        out[...] = piece[...].astype(f32)

    choose(info, pl.program_id(0), refs[:4], info[1], info[2], put)


def swap(value, axis, bit):
    return lax.ppermute(value, axis, [(i, i ^ bit) for i in range(lax.axis_size(axis))])


def shift(value, axis, distance):
    count = lax.axis_size(axis)
    return lax.ppermute(
        value, axis, [(i, i + distance) for i in range(count) if 0 <= i + distance < count]
    )


def part(value, index, rows, axis=0):
    return lax.dynamic_slice_in_dim(value, index * rows, rows, axis)


def add(*terms):
    total = terms[0].astype(f32)
    for term in terms[1:]:
        total = total + term.astype(f32)
    return total.astype(bf16)


def line_states(local, rate, rows, backward):
    count = lax.axis_size("seq")
    sign = -1 if backward else 1
    if count <= 4:
        distances = range(1, count)
        return [shift(local, "seq", sign * d) for d in distances], [d - 1 for d in distances]
    total = shift(local.astype(f32), "seq", sign)
    distance = 1
    while distance < count - 1:
        power = jnp.exp(-rate * rows * distance)[:, None, None]
        total = total + power * shift(total, "seq", sign * distance)
        distance *= 2
    return [total], [0]


class Sum:
    def __init__(self, info, send_a, keep_a, send_b, keep_b):
        self.info, self.keep = info, (keep_a, keep_b)
        self.first = swap(send_a, "dp", 1), swap(send_b, "dp", 2)

    def second(self):
        self.arrived = self.first
        places = 1 - self.info[2], 1 - self.info[1]
        rows = [k.shape[0] // 2 for k in self.keep]
        sent = [
            add(part(k, p, r), part(a, p, r))
            for k, a, p, r in zip(self.keep, self.arrived, places, rows)
        ]
        self.across = swap(sent[0], "dp", 2), swap(sent[1], "dp", 1)
        return sent

    def line(self):
        ins, widths = [], []
        for keep, arrived, across, place in zip(self.keep, self.arrived, self.across, (2, 1)):
            rows, width = across.shape
            spec = pl.BlockSpec((rows, width), lambda i, s, place=place: (s[place], 0))
            ins += [(keep, spec), (arrived, spec), (across, whole(across))]
            widths.append(width)
        self.cut = widths[0]
        shape = rows, sum(widths)
        self.value = call(
            add_quarters,
            1,
            self.info,
            ins,
            [(shape, bf16, pl.BlockSpec(shape, lambda i, s: (0, 0)))],
            name="add_quarters",
        )[0]
        self.four = lax.axis_size("seq") == 4
        if self.four:
            self.inward = lax.ppermute(self.value, "seq", [(0, 1), (3, 2)])
        return self.value

    def line_across(self):
        if self.four:
            self.value = add(self.value, self.inward)
            self.middle = lax.ppermute(self.value, "seq", [(1, 2), (2, 1)])
        return self.value

    def line_back(self):
        if self.four:
            self.total = add(self.value, self.middle)
            self.outer = lax.ppermute(self.total, "seq", [(1, 0), (2, 3)])
        return self.value

    def spread(self):
        if self.four:
            mine = lax.axis_index("seq")
            total = jnp.where((mine == 1) | (mine == 2), self.total, self.outer)
        else:
            total = lax.psum(self.value.astype(f32), "seq").astype(bf16)
        quarters = total[:, : self.cut], total[:, self.cut :]
        self.pieces = []
        for quarter, bit in zip(quarters, (1, 2)):
            second, first = swap(quarter, "dp", 3 ^ bit), swap(quarter, "dp", bit)
            self.pieces.append([quarter, second, first])
        return quarters

    def spread_on(self):
        for pieces, bit in zip(self.pieces, (1, 2)):
            pieces.append(swap(pieces[1], "dp", bit))

    def all_pieces(self):
        return self.pieces[0] + self.pieces[1]


def shards(
    tokens,
    cotangent,
    qkvu_weight,
    out_weight,
    up_weight,
    gate_weight,
    down_weight,
    decay_rate,
    item_length,
    item_slot,
):
    core = lax.axis_index("heads")
    seq_place = lax.axis_index("seq")
    data_place = lax.axis_index("dp")
    block, width = tokens.shape[1:]
    heads = decay_rate.shape[0]
    half = qkvu_weight.shape[2]
    dim = half // heads
    ff = up_weight.shape[1] // 2
    rows = 2 * block
    tile = block // 2
    rate = (decay_rate, SMEM)

    own, own_cot = tokens[0], cotangent[0]
    other = swap(own, "heads", 1)
    other_cot = swap(own_cot, "heads", 1)
    other_out = swap(out_weight, "heads", 1)
    slots = jnp.arange(item_slot.shape[0])
    slot_here = jnp.sum(jnp.where(slots == data_place, item_slot, 0))
    length_here = jnp.sum(jnp.where(slots == slot_here, item_length, 0))
    info = jnp.stack(
        [core, data_place % 2, data_place // 2, length_here - seq_place * rows]
    ).astype(jnp.int32)

    weights = jnp.transpose(qkvu_weight, (1, 0, 2))
    positions = (seq_place * rows + jnp.arange(rows, dtype=jnp.int32)).astype(f32)
    frequency = 10000.0 ** (-jnp.arange(dim // 2, dtype=f32) / (dim // 2))
    angles = positions[:, None] * frequency[None, :]
    cosine, sine = jnp.cos(angles), jnp.sin(angles)
    cs = jnp.concatenate([cosine, cosine], 1)
    sn = jnp.concatenate([-sine, sine], 1)

    def weight(j):
        return weights, pl.BlockSpec((1, width, half), lambda i, s: (j, 0, 0))

    def by(value, size):
        return value, tiles(value, size)

    def all_of(value):
        return value, whole(value)

    def out(columns, kind, size):
        return (rows, columns), kind, pl.BlockSpec((size, columns), lambda i, s: (i, 0))

    def fixed(shape, kind):
        return shape, kind, pl.BlockSpec(shape, lambda i, s: (0,) * len(shape))

    def fn(body, *sizes):
        return functools.partial(body, *sizes)

    square = (heads, dim, dim)
    big, low = pltpu.VMEM((block, half), f32), pltpu.VMEM((block, half), bf16)
    normed, k, v, sk, sv, contrib, local = call(
        fn(project_kv, block, heads, dim),
        2,
        info,
        [all_of(own), all_of(other), weight(1), weight(2), by(cs, block), by(sn, block), rate],
        [out(width, bf16, block)]
        + [out(half, bf16, block)] * 4
        + [fixed((2,) + square, f32), fixed(square, bf16)],
        [big, big, low],
        name="project_kv",
    )
    arrived, powers = line_states(local, decay_rate, rows, False)
    q, sq, u_own, intra = call(
        fn(project_qu, block, heads, dim),
        2,
        info,
        [by(normed, block), weight(0), weight(3), by(cs, block), by(sn, block), rate]
        + [by(k, block), by(v, block)],
        [out(half, bf16, block)] * 3 + [out(half, f32, block)],
        [big],
        after=[local],
        name="project_qu",
    )
    u_other = swap(u_own, "heads", 1)
    halves = pl.BlockSpec((tile, width), lambda i, s: (i % 2, 0))
    g, grad_inner = call(
        fn(begin_back, tile),
        4,
        info,
        [(own_cot, halves), (other_cot, halves)]
        + [(down_weight, pl.BlockSpec((ff, width), lambda i, s: (s[0], 0)))],
        [out(width, bf16, tile), out(ff, bf16, tile)],
        after=[q],
        name="begin_back",
    )
    att_own, states = call(
        fn(attend, block, heads, dim, powers),
        1,
        info,
        [all_of(q), all_of(intra), all_of(contrib), rate] + [all_of(a) for a in arrived],
        [fixed((rows, half), bf16), fixed((2,) + square, bf16)],
        after=[g],
        name="attend",
    )
    att_other = swap(att_own, "heads", 1)
    att_u = [by(att_own, tile), by(att_other, tile), by(u_own, tile), by(u_other, tile)]
    out_both = [all_of(out_weight), all_of(other_out)]
    hidden, n2, mixed = call(
        fn(mix_out, tile),
        4,
        info,
        att_u + out_both + [(own, halves), (other, halves)],
        [out(width, f32, tile), out(width, bf16, tile), out(half, bf16, tile)],
        [pltpu.VMEM((tile, width), bf16)],
        name="mix_out",
    )
    up_spec = pl.BlockSpec((width, ff), lambda i, s: (0, s[0]))
    inner, grad_left, grad_right = call(
        fn(feed, tile),
        4,
        info,
        [by(n2, tile), (up_weight, up_spec), (gate_weight, up_spec), by(grad_inner, tile)],
        [out(ff, bf16, tile)] * 3,
        [pltpu.VMEM((tile, ff), f32)] * 2,
        name="feed",
    )

    def grad(lhs_a, rhs_a, lhs_b, rhs_b, cuts=(None, None), after=(), name=None):
        ins, outs = [], []
        for lhs, rhs, place in ((lhs_a, rhs_a, 1), (lhs_b, rhs_b, 2)):
            size = lhs.shape[1] // 2
            ins += [
                (
                    lhs,
                    pl.BlockSpec(
                        (rows, size),
                        lambda i, s, place=place: (0, jnp.where(i == 0, 1 - s[place], s[place])),
                    ),
                ),
                all_of(rhs),
            ]
            outs += [fixed((size, rhs.shape[1]), bf16)] * 2
        return Sum(
            info, *call(weight_grad, 2, info, ins, outs, after=after, name=name)
        )

    cut = (ff // 128 + 1) // 2 * 128

    def two(value):
        return value[:, :cut], value[:, cut:]

    down_a, down_b = two(inner)
    left_a, left_b = two(grad_left)
    right_a, right_b = two(grad_right)
    down = grad(g, down_a, g, down_b, name="down_grad")
    up = grad(n2, left_a, n2, left_b, after=[down.keep[0]], name="up_grad")
    partial = call(
        back_two,
        4,
        info,
        [by(grad_left, tile), by(grad_right, tile), (up_weight, up_spec), (gate_weight, up_spec)],
        [out(width, bf16, tile)],
        after=[up.keep[0]],
        name="back_two",
    )[0]
    partial_other = swap(partial, "heads", 1)
    gate = grad(n2, right_a, n2, right_b, after=[partial], name="gate_grad")

    turn = pl.BlockSpec(
        (tile, ff), lambda i, s: (jnp.where(i < 2, 2 * (1 - s[0]) + i, 2 * s[0] + i - 2), 0)
    )

    def turned(value):
        return value, pl.BlockSpec(
            (tile, value.shape[1]),
            lambda i, s: (jnp.where(i < 2, 2 * (1 - s[0]) + i, 2 * s[0] + i - 2), 0),
        )

    send_spec = pl.BlockSpec((tile, width), lambda i, s: (jnp.minimum(i, 1), 0))
    keep_spec = pl.BlockSpec((tile, width), lambda i, s: (jnp.maximum(i - 2, 0), 0))
    sides = [((block, width), bf16, send_spec), ((block, width), bf16, keep_spec)]
    send_out, keep_out = call(
        split_product,
        4,
        info,
        [turned(inner), (down_weight, pl.BlockSpec((ff, width), lambda i, s: (s[0], 0)))],
        sides,
        after=[gate.keep[0]],
        name="split_product",
    )
    arrived_out = swap(send_out, "heads", 1)
    dh, branch, dgates, datt, direct, local = call(
        fn(back_mix, tile, block, heads, dim),
        4,
        info,
        [by(partial, tile), by(partial_other, tile), by(hidden, tile), by(g, tile)]
        + att_u
        + out_both
        + [by(q, tile), rate],
        [out(width, f32, tile), out(width, bf16, tile), out(half, bf16, tile), out(half, bf16, tile)]
        + [fixed((2,) + square, f32), fixed(square, bf16)],
        [pltpu.VMEM((tile, half), f32)] * 2 + [pltpu.VMEM((tile, half), bf16)],
        after=[keep_out],
        name="back_mix",
    )
    arrived, powers = line_states(local, decay_rate, rows, True)
    out_u = grad(mixed, branch, normed, dgates, after=[local], name="out_u_grad")
    down_sent = down.second()
    gq, dk, dv = call(
        fn(attend_back, block, heads, dim),
        2,
        info,
        [by(q, block), by(k, block), by(v, block), by(datt, block)]
        + [(states, pl.BlockSpec((1,) + square, lambda i, s: (i, 0, 0, 0))), by(sq, block)]
        + [by(cs, block), by(sn, block), rate],
        [out(half, bf16, block), out(half, f32, block), out(half, f32, block)],
        after=[out_u.keep[0]] + down_sent,
        name="attend_back",
    )
    third = 3 * half // 2
    ga, gb = call(
        fn(finish_back, block, heads, dim, powers),
        2,
        info,
        [by(k, block), by(v, block), by(dk, block), by(dv, block), all_of(direct)]
        + [by(sk, block), by(sv, block), by(cs, block), by(sn, block), rate, by(gq, block)]
        + [all_of(a) for a in arrived],
        [out(third, bf16, block), out(third, bf16, block)],
        [pltpu.VMEM((dim, dim), bf16)],
        name="finish_back",
    )
    qkv = grad(normed, ga, normed, gb, name="qkv_grad")
    up_sent = up.second()
    send_in, keep_in = call(
        back_in,
        4,
        info,
        [turned(dgates), turned(ga), turned(gb), all_of(weights)],
        sides,
        after=[qkv.keep[0]] + up_sent,
        name="back_in",
    )
    arrived_in = swap(send_in, "heads", 1)

    def own_rows(value):
        return part(value, core, block)

    mine = seq_place * rows + core * block + jnp.arange(block, dtype=jnp.int32)
    valid = (mine < length_here).astype(f32)[:, None]
    output = ((own_rows(hidden) + add_wide(keep_out, arrived_out)) * valid).astype(bf16)
    x = own.astype(f32)
    scale = lax.rsqrt(jnp.mean(x * x, axis=-1, keepdims=True) + epsilon)
    dn = add_wide(keep_in, arrived_in)
    grad_inputs = (
        own_rows(dh)
        + scale * dn
        - x * (scale * scale * scale) * jnp.mean(x * dn, axis=-1, keepdims=True)
    )

    gate.second()
    out_u.second()
    qkv.second()
    order = [down, up, gate, out_u, qkv]
    for stage in ("line", "line_across", "line_back", "spread", "spread_on"):
        for sums in order[:3] + order[4:]:
            getattr(sums, stage)()
    finish_apart(out_u)

    def place(body, sums, shape, spec, name):
        pieces = sums if isinstance(sums, list) else sums.all_pieces()
        return call(
            body, 4, info, [all_of(p) for p in pieces], [(shape, f32, spec)], name=name
        )[0]

    flat = pl.BlockSpec((width // 4, ff), lambda i, s: (i, 0))
    return (
        output[None],
        grad_inputs[None],
        place(
            place_heads,
            qkv.all_pieces() + out_u.pieces[1],
            (width, 4, half),
            pl.BlockSpec((width // 4, 4, half), lambda i, s: (i, 0, 0)),
            "place_qkvu",
        ),
        place(
            place_rows,
            out_u.pieces[0],
            (half, width),
            pl.BlockSpec((half // 4, width), lambda i, s: (i, 0)),
            "place_out",
        ),
        place(place_columns, up, (width, ff), flat, "place_up"),
        place(place_columns, gate, (width, ff), flat, "place_gate"),
        place(
            place_turned,
            down,
            (ff, width),
            pl.BlockSpec((ff, width // 4), lambda i, s: (0, i)),
            "place_down",
        ),
    )


def add_wide(a, b):
    return a.astype(f32) + b.astype(f32)


def finish_apart(sums):
    quarters = []
    for keep, arrived, across, place in zip(
        sums.keep, sums.arrived, sums.across, (sums.info[2], sums.info[1])
    ):
        rows = keep.shape[0] // 2
        quarters.append(add(part(keep, place, rows), part(arrived, place, rows), across))
    sums.pieces = []
    for quarter, bit in zip(quarters, (1, 2)):
        total = line_sum(quarter)
        second, first = swap(total, "dp", 3 ^ bit), swap(total, "dp", bit)
        sums.pieces.append([total, second, first, swap(second, "dp", bit)])


def line_sum(value):
    if lax.axis_size("seq") != 4:
        return lax.psum(value.astype(f32), "seq").astype(bf16)
    mine = lax.axis_index("seq")
    value = add(value, lax.ppermute(value, "seq", [(0, 1), (3, 2)]))
    total = add(value, lax.ppermute(value, "seq", [(1, 2), (2, 1)]))
    outer = lax.ppermute(total, "seq", [(1, 0), (2, 3)])
    return jnp.where((mine == 1) | (mine == 2), total, outer)


def solution(mesh):
    placed = (
        P("dp", ("seq", "heads"), None),
        P("dp", ("seq", "heads"), None),
        P(None, None, "heads"),
        P("heads", None),
        P(),
        P(),
        P(),
        P("heads"),
        P(),
        P(),
    )
    return jax.shard_map(
        shards,
        mesh=mesh,
        in_specs=placed,
        out_specs=(
            P("dp", ("seq", "heads"), None),
            P("dp", ("seq", "heads"), None),
            P(None, None, "heads"),
            P("heads", None),
            P(None, "heads"),
            P(None, "heads"),
            P("heads", None),
        ),
        check_vma=False,
    )
```

time: 1100 us -> 545 us (0.50)
  waiting for transfers between devices: 727 us -> 163 us
  Pallas kernels: 0 us -> 215 us
  matrix products: 151 us -> 0 us
  starting transfers between devices: 0.58 us -> 112 us
  local copies, waits for them, and re-layouts: 101 us -> 28.6 us
  blocking collectives: 43.1 us -> 0 us
  other arithmetic: 48.5 us -> 19.2 us
  between operations: 15.7 us -> 2.83 us
    psum x1 -> x0, waiting for transfers between devices: 725 us -> none  [shards(): lax.psum((up_share, gate_share, down_share, out_share, qkvu_share), ('dp'...]
    pallas_call x0 -> x26, Pallas kernels: none -> 215 us  [call(): pl.pallas_call(kernel, grid_spec=pltpu.PrefetchScalarGridSpec(num_scalar_...]
    ppermute x0 -> x82, waiting for transfers between devices: none -> 163 us  [the longest x58 131 us: swap(): lax.ppermute(value, axis, [(i, i ^ bit) for i in range(lax.axis_size(axis...]
    dot_general x35 -> x0, matrix products: 151 us -> none  [the longest x1 11.4 us: shards(): jnp.dot(gathered.T, grad_proj, preferred_element_type=jnp.float32)]
    ppermute x0 -> x82, starting transfers between devices: none -> 112 us  [the longest x58 63.7 us: swap(): lax.ppermute(value, axis, [(i, i ^ bit) for i in range(lax.axis_size(axis...]
    unnamed x96 -> x153, local copies, waits for them, and re-layouts: 46.1 us -> 14.8 us
    all_to_all x4 -> x0, blocking collectives: 29.4 us -> none  [the longest x1 13 us: shards(): lax.all_to_all(grad_arrived, 'heads', split_axis=1, concat_axis=0, tiled=...]
    convert_element_type x9 -> x0, local copies, waits for them, and re-layouts: 13.9 us -> none  [the longest x2 6.81 us: shards(): value_grad_low.astype(jnp.float32)]
  transfers between devices with their start and end apart: 10 -> 82, of which waited for: 2 -> 30; matrix products, arithmetic and copies ran while one was open for 16% -> 6% of each run, Pallas kernels for 0% -> 30%
where the time goes in v1:
time: 545 us; the launch traced here: 540 us
  Pallas kernels  215 us (39%)
  waiting for transfers between devices  163 us (30%)
  starting transfers between devices  112 us (21%)
  local copies, waits for them, and re-layouts  28.6 us (5%)
  other arithmetic  19.2 us (4%)
    pallas_call x26, Pallas kernels, call(): pl.pallas_call(kernel, grid_spec=pltpu.PrefetchScalarGridSpec(num_scalar_...  215 us
    ppermute x58, waiting for transfers between devices, swap(): lax.ppermute(value, axis, [(i, i ^ bit) for i in range(lax.axis_size(axis...  131 us
    ppermute x58, starting transfers between devices, swap(): lax.ppermute(value, axis, [(i, i ^ bit) for i in range(lax.axis_size(axis...  63.7 us
    ppermute x6, starting transfers between devices, shift(): lax.ppermute(value, axis, [(i, i + distance) for i in range(count) if 0 <...  15.4 us
    unnamed x153, local copies, waits for them, and re-layouts  14.8 us
    ppermute x4, waiting for transfers between devices, line_back(): self.outer = lax.ppermute(self.total, 'seq', [(1, 0), (2, 3)])  13.2 us
    ppermute x2, starting transfers between devices, line_sum(): value = add(value, lax.ppermute(value, 'seq', [(0, 1), (3, 2)]))  12.4 us
    ppermute x4, waiting for transfers between devices, line(): self.inward = lax.ppermute(self.value, 'seq', [(0, 1), (3, 2)])  11.7 us
  transfers between devices with their start and end apart: 82, of which 30 were waited for; matrix products, arithmetic and copies ran while one was open for 6% of the time, Pallas kernels for 30%

profile of v1, /device:TPU:0, one launch (start us, length us, event | category | flops | bytes accessed | tf_op | source)
XLA Modules:
  0.0 540.2 jit_solution(16257002462516566864)
XLA Ops:
  12.4 13.9 %project_kv.1 = (bf16[1024,1024]{1,0:T(8,128)(2,1)}, bf16[1024,512]{1,0:T(8,128)(2,1)}, bf16[1024,512]{1,0:T(8,128)(2,1)}, bf16[1024,512]{1,0:T(8,128)(2,1)}, bf...) custom-call(s32[4]{0:T(128)S(1)} %pad_add_fusion.info_ref, ...), custom_call_target="tpu_custom_call" | custom-call | tf_op jit(solution)/shard_map/project_kv/pallas_call | solution.py:46
  37.6 12.6 %project_qu.1 = (bf16[1024,512]{1,0:T(8,128)(2,1)}, bf16[1024,512]{1,0:T(8,128)(2,1)}, bf16[1024,512]{1,0:T(8,128)(2,1)}, f32[1024,512]{1,0:T(8,128)}) custom-call(s32[4]{0:T(128)S(1)} %pad_add_fusion.info_ref, bf16[1024,1024]{1,0:T(8,128)(2,1)} %get-tuple-element.63.refs_0_.refs_2_, bf16[4,1024,512]{2,1,0:T(8,128)(2,1)} %bitcast.20, ...), custom_call_target="tpu_custom_call" | custom-call | tf_op jit(solution)/shard_map/project_qu/pallas_call | solution.py:46
  51.2 8.6 %begin_back.1 = (bf16[1024,1024]{1,0:T(8,128)(2,1)}, bf16[1024,1408]{1,0:T(8,128)(2,1)}) custom-call(s32[4]{0:T(128)S(1)} %pad_add_fusion.info_ref, bf16[512,1024]{1,0:T(8,128)(2,1)S(1)} %bitcast.17, bf16[512,1024]{1,0:T(8,128)(2,1)} %copy-done.49, bf16[2816,1024]{1,0:T(8,128)(2,1)} %refs_1_.3, bf16[1024,512]{1,0:T(8,128)(2,1)} %get-tuple-element.67.refs_3_.refs_0_.refs_10_), custom_call_target="tpu_custom_call" | custom-call | tf_op jit(solution)/shard_map/begin_back/pallas_call | solution.py:46
  68.7 14.4 %mix_out.1 = (f32[1024,1024]{1,0:T(8,128)}, bf16[1024,1024]{1,0:T(8,128)(2,1)}, bf16[1024,512]{1,0:T(8,128)(2,1)S(1)}) custom-call(s32[4]{0:T(128)S(1)} %pad_add_fusion.info_ref, bf16[1024,512]{1,0:T(8,128)(2,1)} %get-tuple-element.71.refs_0_.refs_4_, bf16[1024,512]{1,0:T(8,128)(2,1)} %copy-done.29, bf16[1024,512]{1,0:T(8,128)(2,1)} %get-tuple-element.72.refs_2_.refs_6_, ...), custom_call_target="tpu_custom_call" | custom-call | tf_op jit(solution)/shard_map/mix_out/pallas_call | solution.py:46
  83.1 14.0 %feed.1 = (bf16[1024,1408]{1,0:T(8,128)(2,1)}, bf16[1024,1408]{1,0:T(8,128)(2,1)}, bf16[1024,1408]{1,0:T(8,128)(2,1)}) custom-call(s32[4]{0:T(128)S(1)} %pad_add_fusion.info_ref, bf16[1024,1024]{1,0:T(8,128)(2,1)} %get-tuple-element.74.refs_0_.refs_2_, bf16[1024,2816]{1,0:T(8,128)(2,1)} %refs_2_.5, bf16[1024,2816]{1,0:T(8,128)(2,1)} %refs_3_.3, ...), custom_call_target="tpu_custom_call" | custom-call | tf_op jit(solution)/shard_map/feed/pallas_call | solution.py:46
  104.8 7.8 %down_grad.1 = (bf16[512,768]{1,0:T(8,128)(2,1)}, bf16[512,768]{1,0:T(8,128)(2,1)}, bf16[512,640]{1,0:T(8,128)(2,1)S(1)}, bf16[512,640]{1,0:T(8,128)(2,1)S(1)}) custom-call(s32[4]{0:T(128)S(1)} %pad_add_fusion.info_ref, bf16[1024,1024]{1,0:T(8,128)(2,1)} %get-tuple-element.70.refs_7_.refs_0_.refs_2_.refs_3_, bf16[1024,768]{1,0:T(8,128)(2,1)} %slice.46.refs_1_, ...), custom_call_target="tpu_custom_call" | custom-call | tf_op jit(solution)/shard_map/down_grad/pallas_call | solution.py:46
  113.5 8.0 %up_grad.1 = (bf16[512,768]{1,0:T(8,128)(2,1)}, bf16[512,768]{1,0:T(8,128)(2,1)}, bf16[512,640]{1,0:T(8,128)(2,1)S(1)}, bf16[512,640]{1,0:T(8,128)(2,1)S(1)}) custom-call(s32[4]{0:T(128)S(1)} %pad_add_fusion.info_ref, bf16[1024,1024]{1,0:T(8,128)(2,1)} %get-tuple-element.74.refs_0_.refs_2_, bf16[1024,768]{1,0:T(8,128)(2,1)} %slice.44.refs_1_, ...), custom_call_target="tpu_custom_call" | custom-call | tf_op jit(solution)/shard_map/up_grad/pallas_call | solution.py:46
  124.5 14.0 %collective-permute-done.16.refs_4_ = bf16[512,640]{1,0:T(8,128)(2,1)S(1)} collective-permute-done((bf16[512,640]{1,0:T(8,128)(2,1)S(1)}, bf16[512,640]{1,0:T(8,128)(2,1)S(1)}, u32[]{:S(2)}, u32[]{:S(2)}) %collective-permute-start.16) | collective-permute-done | bytes 655392 | tf_op jit(solution)/shard_map/ppermute | solution.py:482
  141.3 12.1 %back_two.1.refs_4_.refs_0_ = bf16[1024,1024]{1,0:T(8,128)(2,1)} custom-call(s32[4]{0:T(128)S(1)} %pad_add_fusion.info_ref, bf16[1024,1408]{1,0:T(8,128)(2,1)} %get-tuple-element.78.refs_0_, bf16[1024,1408]{1,0:T(8,128)(2,1)} %get-tuple-element.77.refs_1_, bf16[1024,2816]{1,0:T(8,128)(2,1)} %refs_2_.5, bf16[1024,2816]{1,0:T(8,128)(2,1)} %refs_3_.3, ...), custom_call_target="tpu_custom_call" | custom-call | tf_op jit(solution)/shard_map/back_two/pallas_call | solution.py:46
  158.6 7.9 %gate_grad.1 = (bf16[512,768]{1,0:T(8,128)(2,1)}, bf16[512,768]{1,0:T(8,128)(2,1)}, bf16[512,640]{1,0:T(8,128)(2,1)S(1)}, bf16[512,640]{1,0:T(8,128)(2,1)S(1)}) custom-call(s32[4]{0:T(128)S(1)} %pad_add_fusion.info_ref, bf16[1024,1024]{1,0:T(8,128)(2,1)} %get-tuple-element.74.refs_0_.refs_2_, bf16[1024,768]{1,0:T(8,128)(2,1)} %slice.42.refs_1_, ...), custom_call_target="tpu_custom_call" | custom-call | tf_op jit(solution)/shard_map/gate_grad/pallas_call | solution.py:46
  175.3 9.4 %collective-permute-done.60.refs_4_ = bf16[512,640]{1,0:T(8,128)(2,1)S(1)} collective-permute-done((bf16[512,640]{1,0:T(8,128)(2,1)S(1)}, bf16[512,640]{1,0:T(8,128)(2,1)S(1)}, u32[]{:S(2)}, u32[]{:S(2)}) %collective-permute-start.60) | collective-permute-done | bytes 655392 | tf_op jit(solution)/shard_map/ppermute | solution.py:482
  188.6 15.4 %collective-permute-done.10.refs_1_ = bf16[512,768]{1,0:T(8,128)(2,1)S(1)} collective-permute-done((bf16[512,768]{1,0:T(8,128)(2,1)S(1)}, bf16[512,768]{1,0:T(8,128)(2,1)S(1)}, u32[]{:S(2)}, u32[]{:S(2)}) %collective-permute-start.10) | collective-permute-done | bytes 786464 | tf_op jit(solution)/shard_map/ppermute | solution.py:482
  221.1 7.7 %split_product.1 = (bf16[512,1024]{1,0:T(8,128)(2,1)S(1)}, bf16[512,1024]{1,0:T(8,128)(2,1)}) custom-call(s32[4]{0:T(128)S(1)} %pad_add_fusion.info_ref, bf16[1024,1408]{1,0:T(8,128)(2,1)} %get-tuple-element.76.refs_0_, bf16[2816,1024]{1,0:T(8,128)(2,1)} %refs_1_.3, bf16[512,768]{1,0:T(8,128)(2,1)S(1)} %copy-done.5), custom_call_target="tpu_custom_call" | custom-call | tf_op jit(solution)/shard_map/split_product/pallas_call | solution.py:46
  235.2 25.0 %back_mix.1 = (f32[1024,1024]{1,0:T(8,128)}, bf16[1024,1024]{1,0:T(8,128)(2,1)}, bf16[1024,512]{1,0:T(8,128)(2,1)S(1)}, bf16[1024,512]{1,0:T(8,128)(2,1)}, f32[2...) custom-call(s32[4]{0:T(128)S(1)} %pad_add_fusion.info_ref, bf16[1024,1024]{1,0:T(8,128)(2,1)} %back_two.1.refs_4_.refs_0_, ...), custom_call_target="tpu_custom_call" | custom-call | tf_op jit(solution)/shard_map/back_mix/pallas_call | solution.py:46
  274.4 13.4 %attend_back.1 = (bf16[1024,512]{1,0:T(8,128)(2,1)}, f32[1024,512]{1,0:T(8,128)}, f32[1024,512]{1,0:T(8,128)}) custom-call(s32[4]{0:T(128)S(1)} %pad_add_fusion.info_ref, bf16[1024,512]{1,0:T(8,128)(2,1)} %get-tuple-element.67.refs_3_.refs_0_.refs_10_, bf16[1024,512]{1,0:T(8,128)(2,1)} %get-tuple-element.64.refs_6_.refs_1_.refs_0_, ...), custom_call_target="tpu_custom_call" | custom-call | tf_op jit(solution)/shard_map/attend_back/pallas_call | solution.py:46
  288.6 6.4 %finish_back.1 = (bf16[1024,768]{1,0:T(8,128)(2,1)}, bf16[1024,768]{1,0:T(8,128)(2,1)}) custom-call(s32[4]{0:T(128)S(1)} %pad_add_fusion.info_ref, bf16[1024,512]{1,0:T(8,128)(2,1)} %get-tuple-element.64.refs_6_.refs_1_.refs_0_, bf16[1024,512]{1,0:T(8,128)(2,1)} %get-tuple-element.65.refs_7_.refs_2_.refs_1_, f32[1024,512]{1,0:T(8,128)} %get-tuple-element.96.refs_2_, ...), custom_call_target="tpu_custom_call" | custom-call | tf_op jit(solution)/shard_map/finish_back/pallas_call | solution.py:46
  295.1 8.0 %qkv_grad.1 = (bf16[512,768]{1,0:T(8,128)(2,1)S(1)}, bf16[512,768]{1,0:T(8,128)(2,1)S(1)}, bf16[512,768]{1,0:T(8,128)(2,1)}, bf16[512,768]{1,0:T(8,128)(2,1)}) custom-call(s32[4]{0:T(128)S(1)} %pad_add_fusion.info_ref, bf16[1024,1024]{1,0:T(8,128)(2,1)} %get-tuple-element.63.refs_0_.refs_2_, bf16[1024,768]{1,0:T(8,128)(2,1)} %get-tuple-element.102.refs_1_, ...), custom_call_target="tpu_custom_call" | custom-call | tf_op jit(solution)/shard_map/qkv_grad/pallas_call | solution.py:46
  303.1 9.8 %back_in.1 = (bf16[512,1024]{1,0:T(8,128)(2,1)}, bf16[512,1024]{1,0:T(8,128)(2,1)}) custom-call(s32[4]{0:T(128)S(1)} %pad_add_fusion.info_ref, bf16[1024,512]{1,0:T(8,128)(2,1)} %copy-done.6, bf16[1024,768]{1,0:T(8,128)(2,1)} %get-tuple-element.102.refs_1_, bf16[1024,768]{1,0:T(8,128)(2,1)} %get-tuple-element.103.refs_3_.refs_2_, ...), custom_call_target="tpu_custom_call" | custom-call | tf_op jit(solution)/shard_map/back_in/pallas_call | solution.py:46
  318.9 20.6 %collective-permute-done.32 = bf16[256,512]{1,0:T(8,128)(2,1)S(1)} collective-permute-done((bf16[256,512]{1,0:T(8,128)(2,1)S(1)}, bf16[256,512]{1,0:T(8,128)(2,1)S(1)}, u32[]{:S(2)}, u32[]{:S(2)}) %collective-permute-start.32) | collective-permute-done | bytes 262176 | tf_op jit(solution)/shard_map/ppermute | solution.py:482
  341.1 7.8 %collective-permute-start.33 = (bf16[256,512]{1,0:T(8,128)(2,1)S(1)}, bf16[256,512]{1,0:T(8,128)(2,1)S(1)}, u32[]{:S(2)}, u32[]{:S(2)}) collective-permute-start(bf16[256,512]{1,0:T(8,128)(2,1)S(1)} %add_convert_fusion.22), channel_id=1, source_target_pairs={{0,2},{6,4},{1,3},{7,5},{8,10},{14,12},{9,11},{15,13},{16,18},{22,... | collective-permute-start | bytes 786440 | tf_op jit(solution)/shard_map/ppermute | solution.py:918
  360.8 9.1 %collective-permute-done.51 = bf16[256,1408]{1,0:T(8,128)(2,1)S(1)} collective-permute-done((bf16[256,1408]{1,0:T(8,128)(2,1)S(1)}, bf16[256,1408]{1,0:T(8,128)(2,1)S(1)}, u32[]{:S(2)}, u32[]{:S(2)}) %collective-permute-start.51) | collective-permute-done | bytes 720928 | tf_op jit(solution)/shard_map/ppermute | solution.py:565
  387.9 11.7 %collective-permute-done.22 = bf16[256,1536]{1,0:T(8,128)(2,1)S(1)} collective-permute-done((bf16[256,1536]{1,0:T(8,128)(2,1)S(1)}, bf16[256,1536]{1,0:T(8,128)(2,1)S(1)}, u32[]{:S(2)}, u32[]{:S(2)}) %collective-permute-start.22) | collective-permute-done | bytes 786464 | tf_op jit(solution)/shard_map/ppermute | solution.py:553
  433.1 12.2 %collective-permute-done.80.refs_6_ = bf16[256,640]{1,0:T(8,128)(2,1)S(1)} collective-permute-done((bf16[256,640]{1,0:T(8,128)(2,1)S(1)}, bf16[256,640]{1,0:T(8,128)(2,1)S(1)}, u32[]{:S(2)}, u32[]{:S(2)}) %collective-permute-start.80) | collective-permute-done | bytes 327712 | tf_op jit(solution)/shard_map/ppermute | solution.py:482
  533.4 6.5 %place_qkvu.1 = f32[1024,4,512]{2,1,0:T(4,128)} custom-call(s32[4]{0:T(128)S(1)} %pad_add_fusion.info_ref, bf16[256,768]{1,0:T(8,128)(2,1)S(1)} %get-tuple-element.122.refs_0_, bf16[256,768]{1,0:T(8,128)(2,1)S(1)} %collective-permute-done.25.refs_1_, bf16[256,768]{1,0:T(8,128)(2,1)} %copy-done.68, bf16[256,768]{1,0:T(8,128)(2,1)} %collective-permute-done.27.refs_3_, ...), custom_call_target="tpu_custom_call" | custom-call | tf_op jit(solution)/shard_map/place_qkvu/pallas_call | solution.py:46
  (375 shorter events, 261.2 us)
Async XLA Ops:
  1.2 49.1 %collective-permute-start.4 = (bf16[512,1024]{1,0:T(8,128)(2,1)}, bf16[512,1024]{1,0:T(8,128)(2,1)S(1)}, u32[]{:S(2)}, u32[]{:S(2)}) collective-permute-start(bf16[512,1024]{1,0:T(8,128)(2,1)} %bitcast.16), channel_id=1, source_target_pairs={{0,1},{1,0},{2,3},{3,2},{4,5},{5,4},{6,7},{7,6},{8,9},{9,8},{10,11... | collective-permute-start | bytes 3145736 | tf_op jit(solution)/shard_map/ppermute | solution.py:482
  26.3 33.5 %collective-permute-start.1 = (bf16[4,128,128]{2,1,0:T(8,128)(2,1)S(1)}, bf16[4,128,128]{2,1,0:T(8,128)(2,1)S(1)}, u32[]{:S(2)}, u32[]{:S(2)}) collective-permute-start(bf16[4,128,128]{2,1,0:T(8,128)(2,1)S(1)} %get-tuple-element.66.refs_8_), channel_id=1, source_target_pairs={{0,2},{2,4},{4,6},{1,3},{3,5},{5,7},{8,10},{10,12},{12,14},{9,11},... | collective-permute-start | bytes 393224 | tf_op jit(solution)/shard_map/ppermute | solution.py:487
  31.2 28.5 %collective-permute-start.2 = (bf16[4,128,128]{2,1,0:T(8,128)(2,1)S(1)}, bf16[4,128,128]{2,1,0:T(8,128)(2,1)S(1)}, u32[]{:S(2)}, u32[]{:S(2)}) collective-permute-start(bf16[4,128,128]{2,1,0:T(8,128)(2,1)S(1)} %get-tuple-element.66.refs_8_), channel_id=1, source_target_pairs={{0,4},{2,6},{1,5},{3,7},{8,12},{10,14},{9,13},{11,15},{16,20},{18,... | collective-permute-start | bytes 393224 | tf_op jit(solution)/shard_map/ppermute | solution.py:487
  123.0 30.5 %collective-permute-start.15 = (bf16[512,768]{1,0:T(8,128)(2,1)}, bf16[512,768]{1,0:T(8,128)(2,1)}, u32[]{:S(2)}, u32[]{:S(2)}) collective-permute-start(bf16[512,768]{1,0:T(8,128)(2,1)} %get-tuple-element.105), channel_id=1, source_target_pairs={{0,8},{8,0},{16,24},{24,16},{1,9},{9,1},{17,25},{25,17},{2,10},{10... | collective-permute-start | bytes 2359304 | tf_op jit(solution)/shard_map/ppermute | solution.py:482
  138.6 29.0 %collective-permute-start.48 = (bf16[256,640]{1,0:T(8,128)(2,1)S(1)}, bf16[256,640]{1,0:T(8,128)(2,1)S(1)}, u32[]{:S(2)}, u32[]{:S(2)}) collective-permute-start(bf16[256,640]{1,0:T(8,128)(2,1)S(1)} %add_convert_fusion.14.refs_6_), channel_id=1, source_target_pairs={{0,8},{8,0},{16,24},{24,16},{1,9},{9,1},{17,25},{25,17},{2,10},{10... | collective-permute-start | bytes 983048 | tf_op jit(solution)/shard_map/ppermute | solution.py:482
  153.4 81.8 %collective-permute-start.9 = (bf16[1024,1024]{1,0:T(8,128)(2,1)}, bf16[1024,1024]{1,0:T(8,128)(2,1)}, u32[]{:S(2)}, u32[]{:S(2)}) collective-permute-start(bf16[1024,1024]{1,0:T(8,128)(2,1)} %back_two.1.refs_4_.refs_0_), channel_id=1, source_target_pairs={{0,1},{1,0},{2,3},{3,2},{4,5},{5,4},{6,7},{7,6},{8,9},{9,8},{10,11... | collective-permute-start | bytes 6291464 | tf_op jit(solution)/shard_map/ppermute | solution.py:482
  168.3 35.7 %collective-permute-start.10 = (bf16[512,768]{1,0:T(8,128)(2,1)S(1)}, bf16[512,768]{1,0:T(8,128)(2,1)S(1)}, u32[]{:S(2)}, u32[]{:S(2)}) collective-permute-start(bf16[512,768]{1,0:T(8,128)(2,1)S(1)} %copy-done.73), channel_id=1, source_target_pairs={{0,8},{8,0},{16,24},{24,16},{1,9},{9,1},{17,25},{25,17},{2,10},{10... | collective-permute-start | bytes 2359304 | tf_op jit(solution)/shard_map/ppermute | solution.py:482
  169.8 34.8 %collective-permute-start.11 = (bf16[512,640]{1,0:T(8,128)(2,1)S(1)}, bf16[512,640]{1,0:T(8,128)(2,1)S(1)}, u32[]{:S(2)}, u32[]{:S(2)}) collective-permute-start(bf16[512,640]{1,0:T(8,128)(2,1)S(1)} %copy-done.19), channel_id=1, source_target_pairs={{0,16},{8,24},{16,0},{24,8},{1,17},{9,25},{17,1},{25,9},{2,18},{10... | collective-permute-start | bytes 1966088 | tf_op jit(solution)/shard_map/ppermute | solution.py:482
  184.6 48.5 %collective-permute-start.49 = (bf16[256,1408]{1,0:T(8,128)(2,1)}, bf16[256,1408]{1,0:T(8,128)(2,1)}, u32[]{:S(2)}, u32[]{:S(2)}) collective-permute-start(bf16[256,1408]{1,0:T(8,128)(2,1)} %add_quarters.5), channel_id=1, source_target_pairs={{0,2},{6,4},{1,3},{7,5},{8,10},{14,12},{9,11},{15,13},{16,18},{22,... | collective-permute-start | bytes 2162696 | tf_op jit(solution)/shard_map/ppermute | solution.py:553
  219.0 43.9 %collective-permute-start.62 = (bf16[256,1408]{1,0:T(8,128)(2,1)}, bf16[256,1408]{1,0:T(8,128)(2,1)}, u32[]{:S(2)}, u32[]{:S(2)}) collective-permute-start(bf16[256,1408]{1,0:T(8,128)(2,1)} %add_quarters.6), channel_id=1, source_target_pairs={{0,2},{6,4},{1,3},{7,5},{8,10},{14,12},{9,11},{15,13},{16,18},{22,... | collective-permute-start | bytes 2162696 | tf_op jit(solution)/shard_map/ppermute | solution.py:553
  231.8 41.4 %collective-permute-start.73 = (bf16[256,1408]{1,0:T(8,128)(2,1)}, bf16[256,1408]{1,0:T(8,128)(2,1)S(1)}, u32[]{:S(2)}, u32[]{:S(2)}) collective-permute-start(bf16[256,1408]{1,0:T(8,128)(2,1)} %add_quarters.7), channel_id=1, source_target_pairs={{0,2},{6,4},{1,3},{7,5},{8,10},{14,12},{9,11},{15,13},{16,18},{22,... | collective-permute-start | bytes 2162696 | tf_op jit(solution)/shard_map/ppermute | solution.py:553
  234.4 81.1 %collective-permute-start.50 = (bf16[256,1408]{1,0:T(8,128)(2,1)S(1)}, bf16[256,1408]{1,0:T(8,128)(2,1)S(1)}, u32[]{:S(2)}, u32[]{:S(2)}) collective-permute-start(bf16[256,1408]{1,0:T(8,128)(2,1)S(1)} %add_convert_fusion.7), channel_id=1, source_target_pairs={{2,4},{4,2},{3,5},{5,3},{10,12},{12,10},{11,13},{13,11},{18,20},{2... | collective-permute-start | bytes 2162696 | tf_op jit(solution)/shard_map/ppermute | solution.py:559
  273.1 39.7 %collective-permute-start.31 = (bf16[512,512]{1,0:T(8,128)(2,1)S(1)}, bf16[512,512]{1,0:T(8,128)(2,1)S(1)}, u32[]{:S(2)}, u32[]{:S(2)}) collective-permute-start(bf16[512,512]{1,0:T(8,128)(2,1)S(1)} %get-tuple-element.114), channel_id=1, source_target_pairs={{0,16},{8,24},{16,0},{24,8},{1,17},{9,25},{17,1},{25,9},{2,18},{10... | collective-permute-start | bytes 1572872 | tf_op jit(solution)/shard_map/ppermute | solution.py:482
  273.7 40.2 %collective-permute-start.39 = (bf16[256,1024]{1,0:T(8,128)(2,1)S(1)}, bf16[256,1024]{1,0:T(8,128)(2,1)S(1)}, u32[]{:S(2)}, u32[]{:S(2)}) collective-permute-start(bf16[256,1024]{1,0:T(8,128)(2,1)S(1)} %get-tuple-element.115), channel_id=1, source_target_pairs={{0,8},{8,0},{16,24},{24,16},{1,9},{9,1},{17,25},{25,17},{2,10},{10... | collective-permute-start | bytes 1572872 | tf_op jit(solution)/shard_map/ppermute | solution.py:482
  287.8 113.2 %collective-permute-start.8 = (bf16[512,1024]{1,0:T(8,128)(2,1)S(1)}, bf16[512,1024]{1,0:T(8,128)(2,1)}, u32[]{:S(2)}, u32[]{:S(2)}) collective-permute-start(bf16[512,1024]{1,0:T(8,128)(2,1)S(1)} %get-tuple-element.83), channel_id=1, source_target_pairs={{0,1},{1,0},{2,3},{3,2},{4,5},{5,4},{6,7},{7,6},{8,9},{9,8},{10,11... | collective-permute-start | bytes 3145736 | tf_op jit(solution)/shard_map/ppermute | solution.py:482
  287.9 29.5 %collective-permute-start.63 = (bf16[256,1408]{1,0:T(8,128)(2,1)S(1)}, bf16[256,1408]{1,0:T(8,128)(2,1)S(1)}, u32[]{:S(2)}, u32[]{:S(2)}) collective-permute-start(bf16[256,1408]{1,0:T(8,128)(2,1)S(1)} %add_convert_fusion.5), channel_id=1, source_target_pairs={{2,4},{4,2},{3,5},{5,3},{10,12},{12,10},{11,13},{13,11},{18,20},{2... | collective-permute-start | bytes 2162696 | tf_op jit(solution)/shard_map/ppermute | solution.py:559
  313.9 35.1 %collective-permute-start.18 = (bf16[512,768]{1,0:T(8,128)(2,1)S(1)}, bf16[512,768]{1,0:T(8,128)(2,1)S(1)}, u32[]{:S(2)}, u32[]{:S(2)}) collective-permute-start(bf16[512,768]{1,0:T(8,128)(2,1)S(1)} %get-tuple-element.110), channel_id=1, source_target_pairs={{0,8},{8,0},{16,24},{24,16},{1,9},{9,1},{17,25},{25,17},{2,10},{10... | collective-permute-start | bytes 2359304 | tf_op jit(solution)/shard_map/ppermute | solution.py:482
  315.5 34.9 %collective-permute-start.20 = (bf16[512,768]{1,0:T(8,128)(2,1)}, bf16[512,768]{1,0:T(8,128)(2,1)S(1)}, u32[]{:S(2)}, u32[]{:S(2)}) collective-permute-start(bf16[512,768]{1,0:T(8,128)(2,1)} %get-tuple-element.112), channel_id=1, source_target_pairs={{0,16},{8,24},{16,0},{24,8},{1,17},{9,25},{17,1},{25,9},{2,18},{10... | collective-permute-start | bytes 2359304 | tf_op jit(solution)/shard_map/ppermute | solution.py:482
  339.5 66.1 %collective-permute-start.17 = (bf16[512,1024]{1,0:T(8,128)(2,1)}, bf16[512,1024]{1,0:T(8,128)(2,1)S(1)}, u32[]{:S(2)}, u32[]{:S(2)}) collective-permute-start(bf16[512,1024]{1,0:T(8,128)(2,1)} %get-tuple-element.109), channel_id=1, source_target_pairs={{0,1},{1,0},{2,3},{3,2},{4,5},{5,4},{6,7},{7,6},{8,9},{9,8},{10,11... | collective-permute-start | bytes 3145736 | tf_op jit(solution)/shard_map/ppermute | solution.py:482
  386.4 28.7 %collective-permute-start.55 = (bf16[256,640]{1,0:T(8,128)(2,1)S(1)}, bf16[256,640]{1,0:T(8,128)(2,1)S(1)}, u32[]{:S(2)}, u32[]{:S(2)}) collective-permute-start(bf16[256,640]{1,0:T(8,128)(2,1)S(1)} %slice.59.refs_4_), channel_id=1, source_target_pairs={{0,8},{8,0},{16,24},{24,16},{1,9},{9,1},{17,25},{25,17},{2,10},{10... | collective-permute-start | bytes 983048 | tf_op jit(solution)/shard_map/ppermute | solution.py:482
  422.5 28.4 %collective-permute-start.65 = (bf16[256,768]{1,0:T(8,128)(2,1)S(1)}, bf16[256,768]{1,0:T(8,128)(2,1)S(1)}, u32[]{:S(2)}, u32[]{:S(2)}) collective-permute-start(bf16[256,768]{1,0:T(8,128)(2,1)S(1)} %slice.60.refs_0_), channel_id=1, source_target_pairs={{0,16},{8,24},{16,0},{24,8},{1,17},{9,25},{17,1},{25,9},{2,18},{10... | collective-permute-start | bytes 1179656 | tf_op jit(solution)/shard_map/ppermute | solution.py:482
  494.4 38.1 %collective-permute-start.26 = (bf16[256,768]{1,0:T(8,128)(2,1)S(1)}, bf16[256,768]{1,0:T(8,128)(2,1)S(1)}, u32[]{:S(2)}, u32[]{:S(2)}) collective-permute-start(bf16[256,768]{1,0:T(8,128)(2,1)S(1)} %get-tuple-element.122.refs_0_), channel_id=1, source_target_pairs={{0,8},{8,0},{16,24},{24,16},{1,9},{9,1},{17,25},{25,17},{2,10},{10... | collective-permute-start | bytes 1179656 | tf_op jit(solution)/shard_map/ppermute | solution.py:482
  499.4 33.1 %collective-permute-start.29 = (bf16[256,768]{1,0:T(8,128)(2,1)S(1)}, bf16[256,768]{1,0:T(8,128)(2,1)S(1)}, u32[]{:S(2)}, u32[]{:S(2)}) collective-permute-start(bf16[256,768]{1,0:T(8,128)(2,1)S(1)} %get-tuple-element.121.refs_4_), channel_id=1, source_target_pairs={{0,16},{8,24},{16,0},{24,8},{1,17},{9,25},{17,1},{25,9},{2,18},{10... | collective-permute-start | bytes 1179656 | tf_op jit(solution)/shard_map/ppermute | solution.py:482
  499.6 33.0 %collective-permute-start.27 = (bf16[256,768]{1,0:T(8,128)(2,1)S(1)}, bf16[256,768]{1,0:T(8,128)(2,1)}, u32[]{:S(2)}, u32[]{:S(2)}) collective-permute-start(bf16[256,768]{1,0:T(8,128)(2,1)S(1)} %collective-permute-done.25.refs_1_), channel_id=1, source_target_pairs={{0,8},{8,0},{16,24},{24,16},{1,9},{9,1},{17,25},{25,17},{2,10},{10... | collective-permute-start | bytes 1179656 | tf_op jit(solution)/shard_map/ppermute | solution.py:482
  (134 other events, 2157.2 us)
